TPU v7x, 128 devices: a whole 4x4x4 slice. The times are simulated.
128 devices in a mesh: gx: 16 (over z, x), gy: 8 (over y, core).
Axes of the slice: x: 4, y: 4, z: 4, core: 2. Of those that a mesh axis runs over, the one named last changes fastest.
Arguments:
- sea_temp: float32 [2048, 4096], P('gy', 'gx'), may hold values from -1.9 to 1.5
- air_cooling: float32 [2048, 4096], P('gy', 'gx'), may hold values from 0.2 to 2
- ocean_current: float32 [2, 2048, 4096], P(None, 'gy', 'gx'), may hold values from -3 to 3
- wind_stress: float32 [2, 2048, 4096], P(None, 'gy', 'gx'), may hold values from -3 to 3
- land_mask: int32 [2048, 4096], P('gy', 'gx'), may hold values 0 or 1
- velocity: float32 [2, 2048, 4096], P(None, 'gy', 'gx'), may hold values from -2 to 2
- stress: float32 [3, 2048, 4096], P(None, 'gy', 'gx'), may hold values from -3 to 3
- block_owner: int32 [8, 256], P('gy', 'gx'), may hold values from 0 to 15, as said below
- ice_thick: float32 [5, 8, 512, 4096], P(None, 'gy', 'gx'), may hold values from 0.1 to 4
- ice_area: float32 [5, 8, 512, 4096], P(None, 'gy', 'gx'), may hold values from 0.02 to 0.2
- ice_present: int32 [5, 8, 512, 4096], P(None, 'gy', 'gx'), may hold values 0 or 1
Outputs:
- new_thick: float32 [5, 8, 512, 4096], P(None, 'gy', 'gx')
- surface_flux: float32 [2, 2048, 4096], P(None, 'gy', 'gx')
- velocity_out: float32 [2, 2048, 4096], P(None, 'gy', 'gx')
- stress_out: float32 [3, 2048, 4096], P(None, 'gy', 'gx')
Inputs may be any that keep to these rules, and one draw needn't show every extreme that they name: `block_owner`: each entry names an owner in the same gy row; no device names one owner for more than 2 of its blocks.
All inputs are finite; a program needn't handle non-finite values. No bound on the sum of `land_mask` or of `ice_present` on one device may be relied on, other than what follows from the above.
Results may differ from a plain program's by a relative error of at most 0.00012.
Values sent between devices are 32-bit elements; how exact they have to be, the bound alone decides.
A program may use at most 128 MiB of HBM per device.

v0:
```python
import jax
import jax.numpy as jnp
from jax import lax
from jax.sharding import PartitionSpec as P

CAP = 2
NSUB = 8


HIGHEST = lax.Precision.HIGHEST


def extended(block, sides, width):
    for axis, dim in sides:
        count = lax.axis_size(axis)
        forward = [(i, i + 1) for i in range(count - 1)]
        backward = [(target, source) for source, target in forward]
        low = lax.ppermute(
            lax.slice_in_dim(block, block.shape[dim] - width, None, axis=dim), axis, forward
        )
        high = lax.ppermute(lax.slice_in_dim(block, 0, width, axis=dim), axis, backward)
        block = jnp.concatenate([low, block, high], axis=dim)
    return block


def grow_ice(routed_temp, routed_cool, thick_live, area_live):
    basal_flux = 0.5 * (routed_temp + 1.8)
    change = 0.4 * (routed_cool * 0.5 / (thick_live + 0.5) - basal_flux)
    grown = jnp.maximum(thick_live + change, 0.0)
    ice_cover = jnp.sum(area_live, 0)
    ice_mass = jnp.sum(area_live * grown, 0)
    heat_flux = ice_cover * basal_flux - (1.0 - ice_cover) * routed_cool
    fresh_flux = -jnp.sum(area_live * change, 0)
    return (grown, heat_flux, fresh_flux, ice_mass, ice_cover)


def strain_rates(zonal_pad, merid_pad):
    zonal_east = (zonal_pad[1:-1, 2:] - zonal_pad[1:-1, :-2]) * 0.5
    merid_north = (merid_pad[2:, 1:-1] - merid_pad[:-2, 1:-1]) * 0.5
    zonal_north = (zonal_pad[2:, 1:-1] - zonal_pad[:-2, 1:-1]) * 0.5
    merid_east = (merid_pad[1:-1, 2:] - merid_pad[1:-1, :-2]) * 0.5
    return (zonal_east + merid_north, zonal_east - merid_north, zonal_north + merid_east)


def relax_stress(stresses, divergence, tension, shearing, strength):
    deform = jnp.sqrt(
        divergence * divergence + (tension * tension + shearing * shearing) / 4.0 + 0.04
    )
    factor = strength / deform
    new_sum = (stresses[0] + 0.5 * (factor * divergence - strength)) / 1.5
    new_diff = (stresses[1] + 0.5 * factor * tension / 4.0) / 1.5
    new_shear = (stresses[2] + 0.5 * factor * shearing / 4.0) / 1.5
    return jnp.stack([new_sum, new_diff, new_shear])


def move_ice(velocity, stress_pad, wind_stress, ocean_current, inertia, wet_cells):
    along_x = 0.5 * (stress_pad[0] + stress_pad[1])
    along_y = 0.5 * (stress_pad[0] - stress_pad[1])
    shear_pad = stress_pad[2]
    force_east = 0.5 * (along_x[1:-1, 2:] - along_x[1:-1, :-2]) + 0.5 * (
        shear_pad[2:, 1:-1] - shear_pad[:-2, 1:-1]
    )
    force_north = 0.5 * (shear_pad[1:-1, 2:] - shear_pad[1:-1, :-2]) + 0.5 * (
        along_y[2:, 1:-1] - along_y[:-2, 1:-1]
    )
    forces = jnp.stack([force_east, force_north])
    return (
        wet_cells
        * (velocity + 0.3 / inertia * (forces + wind_stress + 0.8 * ocean_current))
        / (1.0 + 0.3 * 0.8 / inertia)
    )


def local(
    sea_temp,
    air_cooling,
    ocean_current,
    wind_stress,
    land_mask,
    velocity,
    stress,
    block_owner,
    ice_thick,
    ice_area,
    ice_present,
):
    row_devices = lax.axis_size("gx")
    own_index = lax.axis_index("gx")
    block_count = block_owner.shape[1]
    rows_dev, cols_dev = sea_temp.shape
    block_cells = rows_dev // block_count * cols_dev
    slot_count = row_devices * CAP
    owners = block_owner[0]
    same_owner = owners[:, None] == owners[None, :]
    earlier = jnp.arange(block_count)[None, :] < jnp.arange(block_count)[:, None]
    block_rank = jnp.sum((same_owner & earlier).astype(jnp.int32), 1)
    target = owners * CAP + block_rank
    select = (jnp.arange(slot_count)[:, None] == target[None, :]).astype(jnp.float32)
    everyone = lax.all_gather(block_owner, "gx", axis=1, tiled=True).reshape(
        row_devices, block_count
    )
    counts = jnp.sum((everyone == own_index).astype(jnp.int32), 1)
    filled = (counts[:, None] > jnp.arange(CAP)[None, :]).reshape(slot_count).astype(jnp.float32)
    present = ice_present[:, 0].astype(jnp.float32)
    thick_live = ice_thick[:, 0] * present
    area_live = ice_area[:, 0] * present
    temp_blocks = sea_temp.reshape(block_count, block_cells)
    cool_blocks = air_cooling.reshape(block_count, block_cells)
    surface = jnp.stack([temp_blocks, cool_blocks], 1).reshape(block_count, 2 * block_cells)
    outgoing = jnp.dot(select, surface, precision=HIGHEST).reshape(
        row_devices, CAP * 2 * block_cells
    )
    incoming = lax.all_to_all(outgoing, "gx", split_axis=0, concat_axis=0, tiled=True).reshape(
        slot_count, 2, block_cells
    )
    grown, heat_flux, fresh_flux, ice_mass, ice_cover = grow_ice(
        incoming[:, 0], incoming[:, 1], thick_live, area_live
    )
    fluxes = jnp.stack([heat_flux, fresh_flux, ice_mass, ice_cover], 1).reshape(
        row_devices, CAP * 4 * block_cells
    )
    returned = lax.all_to_all(fluxes, "gx", split_axis=0, concat_axis=0, tiled=True).reshape(
        slot_count, 4 * block_cells
    )
    per_block = jnp.dot(select.T, returned, precision=HIGHEST).reshape(block_count, 4, block_cells)
    heat_grid = per_block[:, 0].reshape(rows_dev, cols_dev)
    fresh_grid = per_block[:, 1].reshape(rows_dev, cols_dev)
    mass_grid = per_block[:, 2].reshape(rows_dev, cols_dev)
    cover_grid = per_block[:, 3].reshape(rows_dev, cols_dev)
    new_thick = (filled[:, None] * present * grown)[:, None]
    strength = mass_grid * jnp.exp(-2.0 * (1.0 - cover_grid))
    inertia = mass_grid + 0.5
    wet_cells = 1.0 - land_mask.astype(jnp.float32)
    for subcycle in range(NSUB):
        vel_pad = extended(velocity, (("gx", 2), ("gy", 1)), 1)
        divergence, tension, shearing = strain_rates(vel_pad[0], vel_pad[1])
        stress = relax_stress(stress, divergence, tension, shearing, strength)
        stress_pad = extended(stress, (("gx", 2), ("gy", 1)), 1)
        velocity = move_ice(velocity, stress_pad, wind_stress, ocean_current, inertia, wet_cells)
    return (new_thick, jnp.stack([heat_grid, fresh_grid]), velocity, stress)


def solution(mesh):
    return jax.shard_map(
        local,
        mesh=mesh,
        in_specs=(
            P("gy", "gx"),
            P("gy", "gx"),
            P(None, "gy", "gx"),
            P(None, "gy", "gx"),
            P("gy", "gx"),
            P(None, "gy", "gx"),
            P(None, "gy", "gx"),
            P("gy", "gx"),
            P(None, "gy", "gx", None),
            P(None, "gy", "gx", None),
            P(None, "gy", "gx", None),
        ),
        out_specs=(
            P(None, "gy", "gx", None),
            P(None, "gy", "gx"),
            P(None, "gy", "gx"),
            P(None, "gy", "gx"),
        ),
        check_vma=False,
    )
```

profile of v0, /device:TPU:1, one launch (start us, length us, event | category | flops | bytes accessed | tf_op | source)
XLA Modules:
  0.0 488.7 jit_solution(18134416127890018985)
XLA Ops:
  10.7 9.0 %all-to-all-start = ((f32[16,1,16384]{2,1,0:T(1,128)}), f32[16,1,16384]{2,1,0:T(1,128)}, u32[]{:S(2)}, u32[]{:S(2)}) async-start(f32[16,1,16384]{2,1,0:T(1,128)} %all_to_all.16), calls=%async_computation | async-start | bytes 2097152 | tf_op jit(solution)/shard_map/all_to_all | solution.py:113
  23.3 12.4 %all-to-all-done = f32[16,1,16384]{2,1,0:T(1,128)} async-done(((f32[16,1,16384]{2,1,0:T(1,128)}), f32[16,1,16384]{2,1,0:T(1,128)}, u32[]{:S(2)}, u32[]{:S(2)}) %all-to-all-start) | async-done | bytes 1048608 | tf_op jit(solution)/shard_map/all_to_all | solution.py:113
  35.7 4.7 reduce.1
  56.4 4.3 all-to-all-start.1
  65.4 22.7 %collective-permute-done = f32[2,256,1]{2,1,0:T(8,128)S(1)} collective-permute-done((f32[2,256,1]{2,1,0:T(8,128)S(1)}, f32[2,256,1]{2,1,0:T(8,128)S(1)}, u32[]{:S(2)}, u32[]{:S(2)}) %collective-permute-start) | collective-permute-done | bytes 2080 | tf_op jit(solution)/shard_map/ppermute | solution.py:18
  91.1 6.0 %collective-permute-start.2 = (f32[2,1,258]{2,1,0:T(1,128)S(1)}, f32[2,1,258]{2,1,0:T(1,128)S(1)}, u32[]{:S(2)}, u32[]{:S(2)}) collective-permute-start(f32[2,1,258]{2,1,0:T(1,128)S(1)} %get-tuple-element.94), channel_id=1, source_target_pairs={{0,1},{1,2},{2,3},{3,4},{4,5},{5,6},{6,7},{8,9},{9,10},{10,11},{11... | collective-permute-start | bytes 6200 | tf_op jit(solution)/shard_map/ppermute | solution.py:18
  102.4 7.1 %reduce.2 = f32[16,32768]{1,0:T(8,128)} reduce(f32[16,1,32768]{2,1,0:T(1,128)S(1)} %all-to-all-done.1, f32[]{:T(128)} %constant.97), dimensions={1}, to_apply=%all_to_all.15.reduce_sub_computation | reduce | bytes 4194308 | tf_op jit(solution)/shard_map/all_to_all | solution.py:122
  119.7 6.2 %collective-permute-done.4 = f32[3,256,1]{2,1,0:T(8,128)S(1)} collective-permute-done((f32[3,256,1]{2,1,0:T(8,128)S(1)}, f32[3,256,1]{2,1,0:T(8,128)S(1)}, u32[]{:S(2)}, u32[]{:S(2)}) %collective-permute-start.4) | collective-permute-done | bytes 3104 | tf_op jit(solution)/shard_map/ppermute | solution.py:18
  130.2 4.2 collective-permute-start.6
  169.3 6.2 %collective-permute-done.12 = f32[3,256,1]{2,1,0:T(8,128)S(1)} collective-permute-done((f32[3,256,1]{2,1,0:T(8,128)S(1)}, f32[3,256,1]{2,1,0:T(8,128)S(1)}, u32[]{:S(2)}, u32[]{:S(2)}) %collective-permute-start.12) | collective-permute-done | bytes 3104 | tf_op jit(solution)/shard_map/ppermute | solution.py:18
  175.5 4.4 collective-permute-done.13
  180.1 4.2 collective-permute-start.14
  218.4 6.2 %collective-permute-done.20 = f32[3,256,1]{2,1,0:T(8,128)S(1)} collective-permute-done((f32[3,256,1]{2,1,0:T(8,128)S(1)}, f32[3,256,1]{2,1,0:T(8,128)S(1)}, u32[]{:S(2)}, u32[]{:S(2)}) %collective-permute-start.20) | collective-permute-done | bytes 3104 | tf_op jit(solution)/shard_map/ppermute | solution.py:18
  263.9 6.7 %collective-permute-done.28 = f32[3,256,1]{2,1,0:T(8,128)S(1)} collective-permute-done((f32[3,256,1]{2,1,0:T(8,128)S(1)}, f32[3,256,1]{2,1,0:T(8,128)S(1)}, u32[]{:S(2)}, u32[]{:S(2)}) %collective-permute-start.28) | collective-permute-done | bytes 3104 | tf_op jit(solution)/shard_map/ppermute | solution.py:18
  283.1 4.3 collective-permute-start.32
  305.2 4.2 collective-permute-start.36
  310.7 6.7 %collective-permute-done.36 = f32[3,256,1]{2,1,0:T(8,128)S(1)} collective-permute-done((f32[3,256,1]{2,1,0:T(8,128)S(1)}, f32[3,256,1]{2,1,0:T(8,128)S(1)}, u32[]{:S(2)}, u32[]{:S(2)}) %collective-permute-start.36) | collective-permute-done | bytes 3104 | tf_op jit(solution)/shard_map/ppermute | solution.py:18
  356.8 6.7 %collective-permute-done.44 = f32[3,256,1]{2,1,0:T(8,128)S(1)} collective-permute-done((f32[3,256,1]{2,1,0:T(8,128)S(1)}, f32[3,256,1]{2,1,0:T(8,128)S(1)}, u32[]{:S(2)}, u32[]{:S(2)}) %collective-permute-start.44) | collective-permute-done | bytes 3104 | tf_op jit(solution)/shard_map/ppermute | solution.py:18
  399.1 4.5 collective-permute-start.52
  406.1 5.1 %collective-permute-done.52 = f32[3,256,1]{2,1,0:T(8,128)} collective-permute-done((f32[3,256,1]{2,1,0:T(8,128)}, f32[3,256,1]{2,1,0:T(8,128)}, u32[]{:S(2)}, u32[]{:S(2)}) %collective-permute-start.52) | collective-permute-done | bytes 3104 | tf_op jit(solution)/shard_map/ppermute | solution.py:18
  411.2 4.8 collective-permute-done.53
  421.3 11.5 %all-reduce = s32[256]{0:T(256)S(1)} all-reduce(s32[256]{0:T(256)S(1)} %bitcast_dynamic-update-slice_fusion), channel_id=1, replica_groups=mesh['gx'=16,'gy'=8] {'gx'}, use_global_device_ids=true, to_apply=%add | all-reduce | flops 256 | bytes 2048
  446.4 7.9 %collective-permute-start.58 = (f32[2,1,258]{2,1,0:T(1,128)S(1)}, f32[2,1,258]{2,1,0:T(1,128)S(1)}, u32[]{:S(2)}, u32[]{:S(2)}) collective-permute-start(f32[2,1,258]{2,1,0:T(1,128)S(1)} %get-tuple-element.75), channel_id=1, source_target_pairs={{0,1},{1,2},{2,3},{3,4},{4,5},{5,6},{6,7},{8,9},{9,10},{10,11},{11... | collective-permute-start | bytes 6200 | tf_op jit(solution)/shard_map/ppermute | solution.py:18
  473.3 4.4 collective-permute-done.61
  (315 shorter events, 321.2 us)
Async XLA Ops:
  10.7 25.1 %all-to-all-start = ((f32[16,1,16384]{2,1,0:T(1,128)}), f32[16,1,16384]{2,1,0:T(1,128)}, u32[]{:S(2)}, u32[]{:S(2)}) async-start(f32[16,1,16384]{2,1,0:T(1,128)} %all_to_all.16), calls=%async_computation | async-start | bytes 2097152 | tf_op jit(solution)/shard_map/all_to_all | solution.py:113
  56.4 46.0 %all-to-all-start.1 = ((f32[16,1,32768]{2,1,0:T(1,128)}), f32[16,1,32768]{2,1,0:T(1,128)S(1)}, u32[]{:S(2)}, u32[]{:S(2)}) async-start(f32[16,1,32768]{2,1,0:T(1,128)} %all_to_all.17), calls=%async_computation.1 | async-start | bytes 4194304 | tf_op jit(solution)/shard_map/all_to_all | solution.py:122
  60.8 27.3 %collective-permute-start = (f32[2,256,1]{2,1,0:T(8,128)S(1)}, f32[2,256,1]{2,1,0:T(8,128)S(1)}, u32[]{:S(2)}, u32[]{:S(2)}) collective-permute-start(f32[2,256,1]{2,1,0:T(8,128)S(1)} %get-tuple-element.145), channel_id=1, source_target_pairs={{0,8},{8,16},{16,24},{24,32},{32,40},{40,48},{48,56},{56,64},{64,7... | collective-permute-start | bytes 6152 | tf_op jit(solution)/shard_map/ppermute | solution.py:18
  64.1 26.8 %collective-permute-start.1 = (f32[2,256,1]{2,1,0:T(8,128)S(1)}, f32[2,256,1]{2,1,0:T(8,128)S(1)}, u32[]{:S(2)}, u32[]{:S(2)}) collective-permute-start(f32[2,256,1]{2,1,0:T(8,128)S(1)} %get-tuple-element.146), channel_id=1, source_target_pairs={{8,0},{16,8},{24,16},{32,24},{40,32},{48,40},{56,48},{64,56},{72,6... | collective-permute-start | bytes 6152 | tf_op jit(solution)/shard_map/ppermute | solution.py:21
  115.2 10.7 %collective-permute-start.4 = (f32[3,256,1]{2,1,0:T(8,128)S(1)}, f32[3,256,1]{2,1,0:T(8,128)S(1)}, u32[]{:S(2)}, u32[]{:S(2)}) collective-permute-start(f32[3,256,1]{2,1,0:T(8,128)S(1)} %get-tuple-element.129), channel_id=1, source_target_pairs={{0,8},{8,16},{16,24},{24,32},{32,40},{40,48},{48,56},{56,64},{64,7... | collective-permute-start | bytes 9224 | tf_op jit(solution)/shard_map/ppermute | solution.py:18
  118.4 11.6 %collective-permute-start.5 = (f32[3,256,1]{2,1,0:T(8,128)S(1)}, f32[3,256,1]{2,1,0:T(8,128)S(1)}, u32[]{:S(2)}, u32[]{:S(2)}) collective-permute-start(f32[3,256,1]{2,1,0:T(8,128)S(1)} %get-tuple-element.130), channel_id=1, source_target_pairs={{8,0},{16,8},{24,16},{32,24},{40,32},{48,40},{56,48},{64,56},{72,6... | collective-permute-start | bytes 9224 | tf_op jit(solution)/shard_map/ppermute | solution.py:21
  164.2 11.4 %collective-permute-start.12 = (f32[3,256,1]{2,1,0:T(8,128)S(1)}, f32[3,256,1]{2,1,0:T(8,128)S(1)}, u32[]{:S(2)}, u32[]{:S(2)}) collective-permute-start(f32[3,256,1]{2,1,0:T(8,128)S(1)} %get-tuple-element.127), channel_id=1, source_target_pairs={{0,8},{8,16},{16,24},{24,32},{32,40},{40,48},{48,56},{56,64},{64,7... | collective-permute-start | bytes 9224 | tf_op jit(solution)/shard_map/ppermute | solution.py:18
  168.0 11.9 %collective-permute-start.13 = (f32[3,256,1]{2,1,0:T(8,128)S(1)}, f32[3,256,1]{2,1,0:T(8,128)S(1)}, u32[]{:S(2)}, u32[]{:S(2)}) collective-permute-start(f32[3,256,1]{2,1,0:T(8,128)S(1)} %get-tuple-element.128), channel_id=1, source_target_pairs={{8,0},{16,8},{24,16},{32,24},{40,32},{48,40},{56,48},{64,56},{72,6... | collective-permute-start | bytes 9224 | tf_op jit(solution)/shard_map/ppermute | solution.py:21
  213.1 11.5 %collective-permute-start.20 = (f32[3,256,1]{2,1,0:T(8,128)S(1)}, f32[3,256,1]{2,1,0:T(8,128)S(1)}, u32[]{:S(2)}, u32[]{:S(2)}) collective-permute-start(f32[3,256,1]{2,1,0:T(8,128)S(1)} %get-tuple-element.125), channel_id=1, source_target_pairs={{0,8},{8,16},{16,24},{24,32},{32,40},{40,48},{48,56},{56,64},{64,7... | collective-permute-start | bytes 9224 | tf_op jit(solution)/shard_map/ppermute | solution.py:18
  217.1 11.6 %collective-permute-start.21 = (f32[3,256,1]{2,1,0:T(8,128)S(1)}, f32[3,256,1]{2,1,0:T(8,128)S(1)}, u32[]{:S(2)}, u32[]{:S(2)}) collective-permute-start(f32[3,256,1]{2,1,0:T(8,128)S(1)} %get-tuple-element.126), channel_id=1, source_target_pairs={{8,0},{16,8},{24,16},{32,24},{40,32},{48,40},{56,48},{64,56},{72,6... | collective-permute-start | bytes 9224 | tf_op jit(solution)/shard_map/ppermute | solution.py:21
  258.9 11.7 %collective-permute-start.28 = (f32[3,256,1]{2,1,0:T(8,128)S(1)}, f32[3,256,1]{2,1,0:T(8,128)S(1)}, u32[]{:S(2)}, u32[]{:S(2)}) collective-permute-start(f32[3,256,1]{2,1,0:T(8,128)S(1)} %get-tuple-element.123), channel_id=1, source_target_pairs={{0,8},{8,16},{16,24},{24,32},{32,40},{40,48},{48,56},{56,64},{64,7... | collective-permute-start | bytes 9224 | tf_op jit(solution)/shard_map/ppermute | solution.py:18
  262.6 12.1 %collective-permute-start.29 = (f32[3,256,1]{2,1,0:T(8,128)S(1)}, f32[3,256,1]{2,1,0:T(8,128)S(1)}, u32[]{:S(2)}, u32[]{:S(2)}) collective-permute-start(f32[3,256,1]{2,1,0:T(8,128)S(1)} %get-tuple-element.124), channel_id=1, source_target_pairs={{8,0},{16,8},{24,16},{32,24},{40,32},{48,40},{56,48},{64,56},{72,6... | collective-permute-start | bytes 9224 | tf_op jit(solution)/shard_map/ppermute | solution.py:21
  283.1 9.5 %collective-permute-start.32 = (f32[2,256,1]{2,1,0:T(8,128)S(1)}, f32[2,256,1]{2,1,0:T(8,128)S(1)}, u32[]{:S(2)}, u32[]{:S(2)}) collective-permute-start(f32[2,256,1]{2,1,0:T(8,128)S(1)} %get-tuple-element.137), channel_id=1, source_target_pairs={{0,8},{8,16},{16,24},{24,32},{32,40},{40,48},{48,56},{56,64},{64,7... | collective-permute-start | bytes 6152 | tf_op jit(solution)/shard_map/ppermute | solution.py:18
  305.2 12.2 %collective-permute-start.36 = (f32[3,256,1]{2,1,0:T(8,128)S(1)}, f32[3,256,1]{2,1,0:T(8,128)S(1)}, u32[]{:S(2)}, u32[]{:S(2)}) collective-permute-start(f32[3,256,1]{2,1,0:T(8,128)S(1)} %get-tuple-element.121), channel_id=1, source_target_pairs={{0,8},{8,16},{16,24},{24,32},{32,40},{40,48},{48,56},{56,64},{64,7... | collective-permute-start | bytes 9224 | tf_op jit(solution)/shard_map/ppermute | solution.py:18
  309.4 12.1 %collective-permute-start.37 = (f32[3,256,1]{2,1,0:T(8,128)S(1)}, f32[3,256,1]{2,1,0:T(8,128)S(1)}, u32[]{:S(2)}, u32[]{:S(2)}) collective-permute-start(f32[3,256,1]{2,1,0:T(8,128)S(1)} %get-tuple-element.122), channel_id=1, source_target_pairs={{8,0},{16,8},{24,16},{32,24},{40,32},{48,40},{56,48},{64,56},{72,6... | collective-permute-start | bytes 9224 | tf_op jit(solution)/shard_map/ppermute | solution.py:21
  351.7 11.8 %collective-permute-start.44 = (f32[3,256,1]{2,1,0:T(8,128)S(1)}, f32[3,256,1]{2,1,0:T(8,128)S(1)}, u32[]{:S(2)}, u32[]{:S(2)}) collective-permute-start(f32[3,256,1]{2,1,0:T(8,128)S(1)} %get-tuple-element.119), channel_id=1, source_target_pairs={{0,8},{8,16},{16,24},{24,32},{32,40},{40,48},{48,56},{56,64},{64,7... | collective-permute-start | bytes 9224 | tf_op jit(solution)/shard_map/ppermute | solution.py:18
  355.5 12.1 %collective-permute-start.45 = (f32[3,256,1]{2,1,0:T(8,128)S(1)}, f32[3,256,1]{2,1,0:T(8,128)S(1)}, u32[]{:S(2)}, u32[]{:S(2)}) collective-permute-start(f32[3,256,1]{2,1,0:T(8,128)S(1)} %get-tuple-element.120), channel_id=1, source_target_pairs={{8,0},{16,8},{24,16},{32,24},{40,32},{48,40},{56,48},{64,56},{72,6... | collective-permute-start | bytes 9224 | tf_op jit(solution)/shard_map/ppermute | solution.py:21
  399.1 12.1 %collective-permute-start.52 = (f32[3,256,1]{2,1,0:T(8,128)}, f32[3,256,1]{2,1,0:T(8,128)}, u32[]{:S(2)}, u32[]{:S(2)}) collective-permute-start(f32[3,256,1]{2,1,0:T(8,128)} %get-tuple-element.117), channel_id=1, source_target_pairs={{0,8},{8,16},{16,24},{24,32},{32,40},{40,48},{48,56},{56,64},{64,7... | collective-permute-start | bytes 9224 | tf_op jit(solution)/shard_map/ppermute | solution.py:18
  403.6 12.4 %collective-permute-start.53 = (f32[3,256,1]{2,1,0:T(8,128)}, f32[3,256,1]{2,1,0:T(8,128)}, u32[]{:S(2)}, u32[]{:S(2)}) collective-permute-start(f32[3,256,1]{2,1,0:T(8,128)} %get-tuple-element.118), channel_id=1, source_target_pairs={{8,0},{16,8},{24,16},{32,24},{40,32},{48,40},{56,48},{64,56},{72,6... | collective-permute-start | bytes 9224 | tf_op jit(solution)/shard_map/ppermute | solution.py:21
  416.9 15.9 %collective-permute-start.54 = (f32[3,1,258]{2,1,0:T(1,128)S(1)}, f32[3,1,258]{2,1,0:T(1,128)S(1)}, u32[]{:S(2)}, u32[]{:S(2)}) collective-permute-start(f32[3,1,258]{2,1,0:T(1,128)S(1)} %get-tuple-element.29), channel_id=1, source_target_pairs={{0,1},{1,2},{2,3},{3,4},{4,5},{5,6},{6,7},{8,9},{9,10},{10,11},{11... | collective-permute-start | bytes 9296 | tf_op jit(solution)/shard_map/ppermute | solution.py:18
  418.8 14.0 %collective-permute-start.55 = (f32[3,1,258]{2,1,0:T(1,128)S(1)}, f32[3,1,258]{2,1,0:T(1,128)S(1)}, u32[]{:S(2)}, u32[]{:S(2)}) collective-permute-start(f32[3,1,258]{2,1,0:T(1,128)S(1)} %get-tuple-element.30), channel_id=1, source_target_pairs={{1,0},{2,1},{3,2},{4,3},{5,4},{6,5},{7,6},{9,8},{10,9},{11,10},{12... | collective-permute-start | bytes 9296 | tf_op jit(solution)/shard_map/ppermute | solution.py:21
  446.4 10.0 %collective-permute-start.58 = (f32[2,1,258]{2,1,0:T(1,128)S(1)}, f32[2,1,258]{2,1,0:T(1,128)S(1)}, u32[]{:S(2)}, u32[]{:S(2)}) collective-permute-start(f32[2,1,258]{2,1,0:T(1,128)S(1)} %get-tuple-element.75), channel_id=1, source_target_pairs={{0,1},{1,2},{2,3},{3,4},{4,5},{5,6},{6,7},{8,9},{9,10},{10,11},{11... | collective-permute-start | bytes 6200 | tf_op jit(solution)/shard_map/ppermute | solution.py:18
  463.1 10.2 %collective-permute-start.60 = (f32[3,256,1]{2,1,0:T(8,128)}, f32[3,256,1]{2,1,0:T(8,128)S(1)}, u32[]{:S(2)}, u32[]{:S(2)}) collective-permute-start(f32[3,256,1]{2,1,0:T(8,128)} %get-tuple-element.115), channel_id=1, source_target_pairs={{0,8},{8,16},{16,24},{24,32},{32,40},{40,48},{48,56},{56,64},{64,7... | collective-permute-start | bytes 9224 | tf_op jit(solution)/shard_map/ppermute | solution.py:18
  465.5 12.2 %collective-permute-start.61 = (f32[3,256,1]{2,1,0:T(8,128)}, f32[3,256,1]{2,1,0:T(8,128)}, u32[]{:S(2)}, u32[]{:S(2)}) collective-permute-start(f32[3,256,1]{2,1,0:T(8,128)} %get-tuple-element.116), channel_id=1, source_target_pairs={{8,0},{16,8},{24,16},{32,24},{40,32},{48,40},{56,48},{64,56},{72,6... | collective-permute-start | bytes 9224 | tf_op jit(solution)/shard_map/ppermute | solution.py:21
  (73 other events, 443.3 us)
where the time goes:
time: 497 us; the launch traced here: 489 us
  waiting for transfers between devices  208 us (42%)
  starting transfers between devices  178 us (36%)
  other arithmetic  55 us (11%)
  local copies, waits for them, and re-layouts  31 us (6%)
  blocking collectives  11.5 us (2%)
    ppermute x32, starting transfers between devices, extended(): lax.ppermute(lax.slice_in_dim(block, block.shape[dim] - width, None, axis...  108 us
    ppermute x32, waiting for transfers between devices, extended(): lax.ppermute(lax.slice_in_dim(block, 0, width, axis=dim), axis, backward)  105 us
    ppermute x32, waiting for transfers between devices, extended(): lax.ppermute(lax.slice_in_dim(block, block.shape[dim] - width, None, axis...  91 us
    ppermute x32, starting transfers between devices, extended(): lax.ppermute(lax.slice_in_dim(block, 0, width, axis=dim), axis, backward)  56.3 us
    all_to_all x1, waiting for transfers between devices, local(): lax.all_to_all(outgoing, 'gx', split_axis=0, concat_axis=0, tiled=True)  12.4 us
    unnamed x1, blocking collectives  11.5 us
  transfers between devices with their start and end apart: 66, of which 48 were waited for; matrix products, arithmetic and copies ran while one was open for 2% of the time, Pallas kernels for 0%

commit v1 on v0

v1 whole, which is shorter than its diff:
```python
import functools

import jax
import jax.numpy as jnp
from jax import lax
from jax.experimental import pallas as pl
from jax.experimental.pallas import tpu as pltpu
from jax.sharding import PartitionSpec as P

F32 = jnp.float32
MESH = pl.DeviceIdType.MESH
NSUB = 8
NCAT = 5
NBLK = 16
STEPS = (
    (0, 1), (0, 3), (1, 0), (3, 0), (1, 1), (3, 3), (1, 3), (3, 1),
    (2, 2), (0, 2), (2, 0), (1, 2), (2, 1), (3, 2), (2, 3),
)
ROWS = 304
OWN = 24
NO_BLOCK = 1.0e6
U, V, X, Y, H, FU, FV, WET = range(8)


def kernel(
    owner_ref, sea_hbm, air_hbm, cur_hbm, wind_hbm, land_hbm, vel_hbm, str_hbm, thick_hbm, area_hbm, pres_hbm,
    nt_hbm, flux_hbm, velo_hbm, stro_hbm,
    sea, air, thick, area, pres, rc, nt, wind, cur, land,
    snd, rcv, scov, smass, ss1, rcov, rmass, rs1, got,
    S, M, PL, PR, QL, QR, ML, MR, NL, NR, KL, KR, flux,
    cA, cB, cG, cK, outb,
    lsem, osem, snd_s, snd_r, cov_s, cov_r, mass_s, mass_r, s1_s, s1_r, hs, hr, ms, mr,
):
    r = lax.axis_index("gy")
    s = lax.axis_index("gx")
    z, x = s // 4, s % 4

    def dev(dz, dx):
        return ((z + dz) % 4) * 4 + (x + dx) % 4

    loads = {}

    def load(name, src, dst):
        c = pltpu.make_async_copy(src, dst, lsem.at[len(loads)])
        c.start()
        loads[name] = c

    load("sea", sea_hbm, sea)
    load("air", air_hbm, air)
    load("thick", thick_hbm, thick)
    load("area", area_hbm, area)
    load("pres", pres_hbm, pres)
    for t in range(2):
        lanes = pl.ds(t * 128, 128)
        load(("vel", t), vel_hbm.at[:, :, lanes], S.at[pl.ds(U, 2), t, pl.ds(OWN, 256)])
        load(("str", t), str_hbm.at[:, :, lanes], S.at[pl.ds(X, 3), t, pl.ds(OWN, 256)])
        load(("wind", t), wind_hbm.at[:, :, lanes], wind.at[:, t])
        load(("cur", t), cur_hbm.at[:, :, lanes], cur.at[:, t])
        load(("land", t), land_hbm.at[:, lanes], land.at[t])

    barrier = pltpu.get_barrier_semaphore()
    north, south = (r + 1) % 8, (r + 7) % 8
    east, west = (s + 1) % 16, (s + 15) % 16
    for dz, dx in STEPS:
        pl.semaphore_signal(barrier, inc=1, device_id={"gx": dev(dz, dx)}, device_id_type=MESH)
    for ry in (north, south):
        for sx in (west, s, east):
            pl.semaphore_signal(barrier, inc=1, device_id={"gy": ry, "gx": sx}, device_id_type=MESH)

    owners = [owner_ref[0, b] for b in range(NBLK)]
    spare = jnp.zeros((8, 128), F32)
    for f in range(5):
        for t in range(3):
            S[f, t, pl.ds(0, 8), :] = spare
            S[f, t, pl.ds(ROWS - 8, 8), :] = spare

    loads["sea"].wait()
    loads["air"].wait()
    pl.semaphore_wait(barrier, 21)

    def stage(buf, row0, target):
        hits = [(owners[b] == target).astype(jnp.int32) for b in range(NBLK)]
        count = hits[0]
        first = last = hits[0] * 0
        for b in range(1, NBLK):
            first = first + hits[b] * (1 - jnp.minimum(count, 1)) * b
            last = last + hits[b] * (b - last)
            count = count + hits[b]
        for k, b in ((0, first), (1, last)):
            filled = (count > k).astype(jnp.int32).astype(F32)
            temp_b = sea[b] * filled + NO_BLOCK * (1.0 - filled)
            cool_b = air[b]
            for half in range(2):
                at = row0 + k * 64 + half * 16
                buf[pl.ds(at, 16), :] = temp_b[:, half * 128 : half * 128 + 128]
                buf[pl.ds(at + 32, 16), :] = cool_b[:, half * 128 : half * 128 + 128]

    sends = []
    for i, (dz, dx) in enumerate(STEPS):
        target = dev(dz, dx)
        stage(snd, i * 128, target)
        c = pltpu.make_async_remote_copy(
            src_ref=snd.at[pl.ds(i * 128, 128)], dst_ref=rcv.at[pl.ds(pl.multiple_of(s * 128, 128), 128)],
            send_sem=snd_s.at[i], recv_sem=snd_r.at[i], device_id={"gx": target}, device_id_type=MESH,
        )
        c.start()
        sends.append(c)
    stage(rcv, pl.multiple_of(s * 128, 128), s)

    for n in ("thick", "area", "pres"):
        loads[n].wait()

    def prepare(g, row, half):
        lanes = pl.ds(pl.multiple_of(row * 256 + half * 128, 128), 128)
        slots = pl.ds(pl.multiple_of(g * 8, 8), 8)
        cover = jnp.zeros((8, 128), F32)
        s1 = jnp.zeros((8, 128), F32)
        for c in range(NCAT):
            p = pres[c, slots, lanes].astype(F32)
            tl = thick[c, slots, lanes] * p
            al = area[c, slots, lanes] * p
            inv = 1.0 / (tl + 0.5)
            thick[c, slots, lanes] = tl
            area[c, slots, lanes] = al
            rc[c, slots, lanes] = inv
            cover = cover + al
            s1 = s1 + al * inv
        at = g * 256 + half * 16 + row
        scov[pl.ds(at, 8, stride=32), :] = cover
        ss1[pl.ds(at, 8, stride=32), :] = s1

    @pl.loop(0, 64)
    def _(i):
        for half in range(2):
            prepare(i // 16, i % 16, half)

    def back(buf, dst, ssem, rsem, i):
        dz, dx = STEPS[i]
        target = dev(-dz, -dx)
        return pltpu.make_async_remote_copy(
            src_ref=buf.at[pl.ds(pl.multiple_of(target * 64, 64), 64)],
            dst_ref=dst.at[pl.ds(pl.multiple_of(s * 64, 64), 64)],
            send_sem=ssem.at[i], recv_sem=rsem.at[i], device_id={"gx": target}, device_id_type=MESH,
        )

    covs = [back(scov, rcov, cov_s, cov_r, i) for i in range(15)]
    for c in covs:
        c.start()
    mine = pl.ds(pl.multiple_of(s * 64, 64), 64)
    rcov[mine, :] = scov[mine, :]
    rs1[mine, :] = ss1[mine, :]

    for t in range(2):
        for n in ("vel", "str", "wind", "cur", "land"):
            loads[(n, t)].wait()

    lane = lax.broadcasted_iota(jnp.int32, (8, 128), 1)
    own_rows = lambda i: pl.ds(pl.multiple_of(OWN + i * 8, 8), 8)

    @pl.loop(0, 32)
    def _(i):
        at = own_rows(i)
        raw = pl.ds(pl.multiple_of(i * 8, 8), 8)
        fields = []
        for t in range(2):
            total, diff = S[X, t, at, :], S[Y, t, at, :]
            S[X, t, at, :] = total + diff
            S[Y, t, at, :] = total - diff
            S[H, t, at, :] = 2.0 * S[H, t, at, :]
            S[FU, t, at, :] = wind[0, t, raw, :] + 0.8 * cur[0, t, raw, :]
            S[FV, t, at, :] = wind[1, t, raw, :] + 0.8 * cur[1, t, raw, :]
            S[WET, t, at, :] = 1.0 - land[t, raw, :].astype(F32)
        left = S[0, 0, at, :]
        right = pltpu.roll(S[0, 1, at, :], 16, 1)
        for f in range(1, 8):
            here = (lane >= 16 * f) & (lane < 16 * f + 16)
            left = jnp.where(here, pltpu.roll(S[f, 0, at, :], 16 * f, 1), left)
            last = S[f, 1, at, :]
            right = jnp.where(here, pltpu.roll(last, 16 * f + 16, 1) if f < 7 else last, right)
        PL[raw, :] = left
        PR[raw, :] = right

    first16, last16 = pl.ds(OWN, 16), pl.ds(OWN + 240, 16)
    above, below = pl.ds(280, 16), pl.ds(8, 16)

    def remote(src, dst, sems, n, to):
        return pltpu.make_async_remote_copy(
            src_ref=src, dst_ref=dst, send_sem=sems[0].at[n], recv_sem=sems[1].at[n],
            device_id=to, device_id_type=MESH,
        )

    two = pl.ds(0, 2)
    sems = (hs, hr)
    halo = [
        remote(PL, QR.at[pl.ds(16, 256)], sems, 0, {"gx": west}),
        remote(PR, QL.at[pl.ds(16, 256)], sems, 1, {"gx": east}),
        remote(S.at[:, two, first16], S.at[:, two, above], sems, 2, {"gy": south}),
        remote(S.at[:, two, last16], S.at[:, two, below], sems, 3, {"gy": north}),
        remote(PL.at[pl.ds(0, 16)], QR.at[pl.ds(272, 16)], sems, 4, {"gy": south, "gx": west}),
        remote(PR.at[pl.ds(0, 16)], QL.at[pl.ds(272, 16)], sems, 5, {"gy": south, "gx": east}),
        remote(PL.at[pl.ds(240, 16)], QR.at[pl.ds(0, 16)], sems, 6, {"gy": north, "gx": west}),
        remote(PR.at[pl.ds(240, 16)], QL.at[pl.ds(0, 16)], sems, 7, {"gy": north, "gx": east}),
    ]
    for c in halo:
        c.start()

    stores = []
    masses = [back(smass, rmass, mass_s, mass_r, i) for i in range(15)]

    for dz in range(4):
        group = (z + 4 - dz) % 4
        for i in range(15):
            if STEPS[i][0] == dz:
                sends[i].wait_recv()

        def grow(row, half):
            lanes = pl.ds(pl.multiple_of(row * 256 + half * 128, 128), 128)
            slots = pl.ds(pl.multiple_of(group * 8, 8), 8)
            at = group * 512 + half * 16 + row
            heat_in = 0.2 * (rcv[pl.ds(at, 8, stride=64), :] + 1.8)
            cool_in = 0.2 * rcv[pl.ds(at + 32, 8, stride=64), :]
            mass = jnp.zeros((8, 128), F32)
            for c in range(NCAT):
                change = cool_in * rc[c, slots, lanes] - heat_in
                grown = jnp.maximum(thick[c, slots, lanes] + change, 0.0)
                mass = mass + area[c, slots, lanes] * grown
                nt[c, slots, lanes] = pres[c, slots, lanes].astype(F32) * grown
            smass[pl.ds(group * 256 + half * 16 + row, 8, stride=32), :] = mass

        @pl.loop(0, 16)
        def _(row):
            for half in range(2):
                grow(row, half)

        for i in range(15):
            if STEPS[i][0] == dz:
                masses[i].start()
        slots = pl.ds(pl.multiple_of(group * 8, 8), 8)
        c = pltpu.make_async_copy(nt.at[:, slots], nt_hbm.at[:, slots], osem.at[dz])
        c.start()
        stores.append(c)
    rmass[mine, :] = smass[mine, :]
    s1s = [back(ss1, rs1, s1_s, s1_r, i) for i in range(15)]

    at_west, at_east = s == 0, s == 15
    at_south, at_north = r == 0, r == 7
    for c in halo:
        c.wait_recv()

    def beside(right, left, shift_right, shift_left):
        a = jnp.where(at_east, 0.0, pltpu.roll(right, shift_right, 1) if shift_right else right)
        b = jnp.where(at_west, 0.0, pltpu.roll(left, shift_left, 1) if shift_left else left)
        return jnp.where(lane < 16, a, jnp.where(lane >= 112, b, 0.0))

    @pl.loop(0, 36)
    def _(i):
        raw = pl.ds(pl.multiple_of(i * 8, 8), 8)
        at = pl.ds(pl.multiple_of(i * 8 + 8, 8), 8)
        right, left = QR[raw, :], QL[raw, :]
        for f in range(8):
            S[f, 2, at, :] = beside(right, left, (128 - 16 * f) % 128, (112 - 16 * f) % 128)

    def clear_outside(ref, n):
        for at, gone in ((below, at_south), (above, at_north)):
            for f in range(n):
                for t in range(3):
                    ref[f, t, at, :] = jnp.where(gone, 0.0, ref[f, t, at, :])

    clear_outside(S, 8)

    slot_of = []
    for b in range(NBLK):
        slot = owners[b] * 2
        for e in range(b):
            slot = slot + (owners[e] == owners[b]).astype(jnp.int32)
        slot_of.append(slot)
    for c in covs:
        c.wait_recv()
    for c in masses:
        c.wait_recv()
    for k in range(32):
        got[0, k] = rmass[pl.ds(k * 32, 32), :]
        got[1, k] = rcov[pl.ds(k * 32, 32), :]
    for b in range(NBLK):
        mass, cover = got[0, slot_of[b]], got[1, slot_of[b]]
        strength = mass * jnp.exp(-2.0 * (1.0 - cover))
        temp_b, cool_b = sea[b], air[b]
        for half in range(2):
            part = slice(half * 16, half * 16 + 16)
            lanes = slice(half * 128, half * 128 + 128)
            M[0, half, pl.ds(OWN + b * 16, 16), :] = mass[part]
            M[1, half, pl.ds(OWN + b * 16, 16), :] = strength[part]
            cv = cover[part]
            flux[0, half, pl.ds(b * 16, 16), :] = cv * (0.5 * (temp_b[:, lanes] + 1.8)) - (1.0 - cv) * cool_b[:, lanes]

    for i in range(8):
        left = jnp.zeros((8, 128), F32)
        right = left
        for chunk in range(4):
            for f in range(2):
                at = pl.ds(OWN + chunk * 64 + i * 8, 8)
                k = 32 * chunk + 16 * f
                here = (lane >= k) & (lane < k + 16)
                a, b = M[f, 0, at, :], M[f, 1, at, :]
                left = jnp.where(here, pltpu.roll(a, k, 1) if k else a, left)
                right = jnp.where(here, pltpu.roll(b, (k + 16) % 128, 1) if k != 112 else b, right)
        ML[pl.ds(i * 8, 8), :] = left
        MR[pl.ds(i * 8, 8), :] = right
    sems = (ms, mr)
    halo_m = [
        remote(ML, NR, sems, 0, {"gx": west}),
        remote(MR, NL, sems, 1, {"gx": east}),
        remote(M.at[:, two, first16], M.at[:, two, above], sems, 2, {"gy": south}),
        remote(M.at[:, two, last16], M.at[:, two, below], sems, 3, {"gy": north}),
        remote(ML.at[pl.ds(0, 16)], KR.at[1], sems, 4, {"gy": south, "gx": west}),
        remote(MR.at[pl.ds(0, 16)], KL.at[1], sems, 5, {"gy": south, "gx": east}),
        remote(ML.at[pl.ds(48, 16)], KR.at[0], sems, 6, {"gy": north, "gx": west}),
        remote(MR.at[pl.ds(48, 16)], KL.at[0], sems, 7, {"gy": north, "gx": east}),
    ]
    for c in halo_m:
        c.start()
    for c in s1s:
        c.start()
    for c in halo_m:
        c.wait_recv()
    for f in range(2):
        for chunk in range(4):
            k = 32 * chunk + 16 * f
            for i in range(8):
                at = pl.ds(OWN + chunk * 64 + i * 8, 8)
                raw = pl.ds(i * 8, 8)
                M[f, 2, at, :] = beside(NR[raw, :], NL[raw, :], (128 - k) % 128, (112 - k) % 128)
        for i in range(2):
            raw = pl.ds(i * 8, 8)
            k = 96 + 16 * f
            M[f, 2, pl.ds(8 + i * 8, 8), :] = beside(KR[0, raw, :], KL[0, raw, :], 128 - k, (112 - k) % 128)
            k = 16 * f
            M[f, 2, pl.ds(280 + i * 8, 8), :] = beside(KR[1, raw, :], KL[1, raw, :], (128 - k) % 128, 112 - k)
    clear_outside(M, 2)

    @pl.loop(1, 37)
    def _(i):
        at = pl.ds(pl.multiple_of(i * 8, 8), 8)
        for t in range(3):
            inertia = M[0, t, at, :] + 0.5
            w = S[WET, t, at, :] / (inertia + 0.24)
            cA[t, at, :] = w * inertia
            cB[t, at, :] = 0.075 * w
            cG[0, t, at, :] = 0.3 * w * S[FU, t, at, :]
            cG[1, t, at, :] = 0.3 * w * S[FV, t, at, :]
            cK[t, at, :] = M[1, t, at, :] * (1.0 / 6.0)

    for c in halo:
        c.wait_send()
    R = 8
    wide = lax.broadcasted_iota(jnp.int32, (R, 128), 1)
    is_last, is_first = wide == 127, wide == 0

    def across(f, at):
        v = [S[f, t, at, :] for t in range(3)]
        up = [pltpu.roll(a, 127, 1) for a in v]
        down = [pltpu.roll(a, 1, 1) for a in v]
        return [
            jnp.where(is_last, up[(t + 1) % 3], up[t]) - jnp.where(is_first, down[(t + 2) % 3], down[t])
            for t in range(3)
        ]

    def along(f, t, row0):
        return S[f, t, pl.ds(row0 + 1, R), :] - S[f, t, pl.ds(row0 - 1, R), :]

    @pl.loop(0, NSUB)
    def _(n):
        @pl.loop(0, 288 // R)
        def _(i):
            row0 = pl.multiple_of(i * R + 8, 8)
            at = pl.ds(row0, R)
            ux, vx = across(U, at), across(V, at)
            for t in range(3):
                a, b = ux[t], along(V, t, row0)
                sh = along(U, t, row0) + vx[t]
                d, e = a + b, a - b
                k = cK[t, at, :]
                d4 = 4.0 * d
                q = d * d4 + e * e + (sh * sh + 0.64)
                f = k * lax.rsqrt(q)
                k2 = k + k
                S[X, t, at, :] = S[X, t, at, :] * (1.0 / 1.5) + (f * (d4 + e) - k2)
                S[Y, t, at, :] = S[Y, t, at, :] * (1.0 / 1.5) + (f * (d4 - e) - k2)
                S[H, t, at, :] = S[H, t, at, :] * (1.0 / 1.5) + (f + f) * sh

        @pl.loop(0, 288 // R)
        def _(i):
            row0 = pl.multiple_of(i * R + 8, 8)
            at = pl.ds(row0, R)
            xx, hx = across(X, at), across(H, at)
            for t in range(3):
                a, b = cA[t, at, :], cB[t, at, :]
                fe = xx[t] + along(H, t, row0)
                fn = hx[t] + along(Y, t, row0)
                S[U, t, at, :] = a * S[U, t, at, :] + (b * fe + cG[0, t, at, :])
                S[V, t, at, :] = a * S[V, t, at, :] + (b * fn + cG[1, t, at, :])

    @pl.loop(0, 32)
    def _(i):
        at = own_rows(i)
        raw = pl.ds(pl.multiple_of(i * 8, 8), 8)
        for t in range(2):
            a, b = S[X, t, at, :], S[Y, t, at, :]
            outb[0, t, raw, :] = 0.5 * (a + b)
            outb[1, t, raw, :] = 0.5 * (a - b)
            outb[2, t, raw, :] = 0.5 * S[H, t, at, :]

    def store(src, dst):
        c = pltpu.make_async_copy(src, dst, osem.at[len(stores)])
        c.start()
        stores.append(c)

    for t in range(2):
        lanes = pl.ds(t * 128, 128)
        store(S.at[pl.ds(U, 2), t, pl.ds(OWN, 256)], velo_hbm.at[:, :, lanes])
        store(outb.at[:, t], stro_hbm.at[:, :, lanes])

    for c in s1s:
        c.wait_recv()
    for k in range(32):
        got[2, k] = rs1[pl.ds(k * 32, 32), :]
    for b in range(NBLK):
        s1, cover = got[2, slot_of[b]], got[1, slot_of[b]]
        temp_b, cool_b = sea[b], air[b]
        for half in range(2):
            part = slice(half * 16, half * 16 + 16)
            lanes = slice(half * 128, half * 128 + 128)
            basal = 0.5 * (temp_b[:, lanes] + 1.8)
            flux[1, half, pl.ds(b * 16, 16), :] = 0.4 * (basal * cover[part] - 0.5 * cool_b[:, lanes] * s1[part])
    for t in range(2):
        store(flux.at[:, t], flux_hbm.at[:, :, pl.ds(t * 128, 128)])
    for c in sends + covs + masses + s1s + halo_m:
        c.wait_send()
    for c in stores:
        c.wait()


def local(sea, air, cur, wind, land, vel, stress, owner, thick, area, pres):
    any_ = pl.BlockSpec(memory_space=pl.ANY)
    vm = lambda *shape, dtype=F32: pltpu.VMEM(shape, dtype)
    dma = lambda n: pltpu.SemaphoreType.DMA((n,))
    nt, flux, velo, stro = pl.pallas_call(
        kernel,
        out_shape=(
            jax.ShapeDtypeStruct((NCAT, 32, 4096), F32),
            jax.ShapeDtypeStruct((2, 256, 256), F32),
            jax.ShapeDtypeStruct((2, 256, 256), F32),
            jax.ShapeDtypeStruct((3, 256, 256), F32),
        ),
        in_specs=[pl.BlockSpec(memory_space=pltpu.SMEM)] + [any_] * 10,
        out_specs=(any_,) * 4,
        scratch_shapes=[
            vm(16, 16, 256), vm(16, 16, 256),
            vm(NCAT, 32, 4096), vm(NCAT, 32, 4096), vm(NCAT, 32, 4096, dtype=jnp.int32),
            vm(NCAT, 32, 4096), vm(NCAT, 32, 4096),
            vm(2, 2, 256, 128), vm(2, 2, 256, 128), vm(2, 256, 128, dtype=jnp.int32),
            vm(15 * 128, 128), vm(16 * 128, 128),
            vm(1024, 128), vm(1024, 128), vm(1024, 128),
            vm(1024, 128), vm(1024, 128), vm(1024, 128), vm(3, 32, 32, 128),
            vm(8, 3, ROWS, 128), vm(2, 3, ROWS, 128),
            vm(256, 128), vm(256, 128), vm(288, 128), vm(288, 128),
            vm(64, 128), vm(64, 128), vm(64, 128), vm(64, 128), vm(2, 16, 128), vm(2, 16, 128),
            vm(2, 2, 256, 128),
            vm(3, ROWS, 128), vm(3, ROWS, 128), vm(2, 3, ROWS, 128), vm(3, ROWS, 128),
            vm(3, 2, 256, 128),
            dma(15), dma(10),
            dma(15), dma(15), dma(15), dma(15), dma(15), dma(15), dma(15), dma(15),
            dma(8), dma(8), dma(8), dma(8),
        ],
        compiler_params=pltpu.CompilerParams(
            collective_id=0, has_side_effects=True, vmem_limit_bytes=48 * 1024 * 1024
        ),
    )(
        owner, sea.reshape(16, 16, 256), air.reshape(16, 16, 256), cur, wind, land, vel, stress,
        thick.reshape(NCAT, 32, 4096), area.reshape(NCAT, 32, 4096), pres.reshape(NCAT, 32, 4096),
    )
    return nt.reshape(NCAT, 1, 32, 4096), flux, velo, stro


def solution(mesh):
    grid, pair, ice = P("gy", "gx"), P(None, "gy", "gx"), P(None, "gy", "gx", None)
    return jax.shard_map(
        local,
        mesh=mesh,
        in_specs=(grid, grid, pair, pair, grid, pair, pair, grid, ice, ice, ice),
        out_specs=(ice, pair, pair, pair),
        check_vma=False,
    )
```

time: 497 us -> 119 us (0.24); the launches traced: 489 us -> 118 us
  waiting for transfers between devices: 208 us -> 0 us
  starting transfers between devices: 178 us -> 0 us
  Pallas kernels: 0 us -> 103 us
  other arithmetic: 55 us -> 0 us
  local copies, waits for them, and re-layouts: 31 us -> 13.7 us
  blocking collectives: 11.5 us -> 0 us
    ppermute x64 -> x0, waiting for transfers between devices: 196 us -> none  [the longest x32 105 us: extended(): lax.ppermute(lax.slice_in_dim(block, 0, width, axis=dim), axis, backward)]
    ppermute x64 -> x0, starting transfers between devices: 164 us -> none  [the longest x32 108 us: extended(): lax.ppermute(lax.slice_in_dim(block, block.shape[dim] - width, None, axis...]
    pallas_call x0 -> x1, Pallas kernels: none -> 103 us  [local(): pl.pallas_call(kernel, out_shape=(jax.ShapeDtypeStruct((NCAT, 32, 4096),...]
    all_to_all x2 -> x0, starting transfers between devices: 13.3 us -> none  [the longest x1 9.02 us: local(): lax.all_to_all(outgoing, 'gx', split_axis=0, concat_axis=0, tiled=True)]
    all_to_all x2 -> x0, waiting for transfers between devices: 12.4 us -> none  [the longest x1 12.4 us: local(): lax.all_to_all(outgoing, 'gx', split_axis=0, concat_axis=0, tiled=True)]
    all_to_all x2 -> x0, other arithmetic: 11.8 us -> none  [the longest x1 7.09 us: local(): lax.all_to_all(fluxes, 'gx', split_axis=0, concat_axis=0, tiled=True)]
    unnamed x1 -> x0, blocking collectives: 11.5 us -> none
    div x23 -> x0, other arithmetic: 10.6 us -> none  [the longest x7 4.61 us: relax_stress(): new_sum = (stresses[0] + 0.5 * (factor * divergence - strength)) / 1.5]
  transfers between devices with their start and end apart: 66 -> 0, of which waited for: 48 -> 0; matrix products, arithmetic and copies ran while one was open for 2% -> 0% of each run, Pallas kernels for 0% -> 0%
where the time goes in v1:
time: 119 us; the launch traced here: 118 us
  Pallas kernels  103 us (87%)
  local copies, waits for them, and re-layouts  13.7 us (12%)
    pallas_call x1, Pallas kernels, local(): pl.pallas_call(kernel, out_shape=(jax.ShapeDtypeStruct((NCAT, 32, 4096),...  103 us
    unnamed x20, local copies, waits for them, and re-layouts  13.7 us

profile of v1, /device:TPU:1, one launch (start us, length us, event | category | flops | bytes accessed | tf_op | source)
XLA Modules:
  0.0 117.9 jit_solution(8546683918649160591)
XLA Ops:
  0.6 0.0 copy-start
  0.6 1.1 copy-done
  1.8 0.0 copy-start.1
  1.8 1.0 copy-done.1
  2.8 0.0 copy-start.2
  2.8 1.0 copy-done.2
  3.9 0.0 copy-start.3
  3.9 1.0 copy-done.3
  4.9 0.0 copy-start.4
  4.9 0.9 copy-done.4
  5.8 0.0 copy-start.5
  5.8 0.9 copy-done.5
  6.8 0.0 copy-start.6
  6.8 0.9 copy-done.6
  7.7 0.0 copy-start.7
  7.7 0.7 copy-done.7
  8.4 103.5 %shard_map.138 = (f32[5,32,4096]{2,1,0:T(8,128)}, f32[2,256,256]{2,1,0:T(8,128)S(1)}, f32[2,256,256]{2,1,0:T(8,128)S(1)}, f32[3,256,256]{2,1,0:T(8,128)S(1)}) custom-call(s32[1,16]{1,0:T(1,128)S(1)} %copy-done.7, f32[16,16,256]{2,1,0:T(8,128)S(1)} %bitcast.8, f32[16,16,256]{2,1,0:T(8,128)S(1)} %bitcast.9, f32[2,256,256]{2,1,0:T(8,128)S(1)} %copy-done.1, ...), custom_call_target="tpu_custom_call" | custom-call | tf_op jit(solution)/shard_map/pallas_call | solution.py:447
  111.9 3.5 %copy.20 = f32[5,1,32,4096]{3,2,1,0:T(8,128)} copy(f32[5,1,32,4096]{3,2,1,0:T(8,128)} %bitcast.10) | data formatting | bytes 5242880
  115.4 0.8 copy.21
  116.2 0.8 copy.22
  117.0 0.9 copy.23
Async XLA Ops:
  0.6 1.1 copy-start
  1.8 1.0 copy-start.1
  2.8 1.0 copy-start.2
  3.9 1.0 copy-start.3
  4.9 0.9 copy-start.4
  5.8 0.9 copy-start.5
  6.8 0.9 copy-start.6
  7.7 0.7 copy-start.7

commit v2 on v1

--- a/solution.py
+++ b/solution.py
@@ -13,8 +13,8 @@
 NCAT = 5
 NBLK = 16
 STEPS = (
-    (0, 1), (0, 3), (1, 0), (3, 0), (1, 1), (3, 3), (1, 3), (3, 1),
-    (2, 2), (0, 2), (2, 0), (1, 2), (2, 1), (3, 2), (2, 3),
+    (1, 2), (0, 2), (2, 1), (2, 0), (3, 2), (0, 1), (2, 3), (1, 0),
+    (2, 2), (0, 3), (1, 1), (3, 0), (3, 3), (1, 3), (3, 1),
 )
 ROWS = 304
 OWN = 24
@@ -35,7 +35,10 @@
     s = lax.axis_index("gx")
     z, x = s // 4, s % 4
 
+    odd = r % 2
+
     def dev(dz, dx):
+        dz, dx = dz + odd * (dx - dz), dx + odd * (dz - dx)
         return ((z + dz) % 4) * 4 + (x + dx) % 4
 
     loads = {}
@@ -76,7 +79,6 @@
 
     loads["sea"].wait()
     loads["air"].wait()
-    pl.semaphore_wait(barrier, 21)
 
     def stage(buf, row0, target):
         hits = [(owners[b] == target).astype(jnp.int32) for b in range(NBLK)]
@@ -95,10 +97,12 @@
                 buf[pl.ds(at, 16), :] = temp_b[:, half * 128 : half * 128 + 128]
                 buf[pl.ds(at + 32, 16), :] = cool_b[:, half * 128 : half * 128 + 128]
 
+    for i, (dz, dx) in enumerate(STEPS):
+        stage(snd, i * 128, dev(dz, dx))
+    pl.semaphore_wait(barrier, 21)
     sends = []
     for i, (dz, dx) in enumerate(STEPS):
         target = dev(dz, dx)
-        stage(snd, i * 128, target)
         c = pltpu.make_async_remote_copy(
             src_ref=snd.at[pl.ds(i * 128, 128)], dst_ref=rcv.at[pl.ds(pl.multiple_of(s * 128, 128), 128)],
             send_sem=snd_s.at[i], recv_sem=snd_r.at[i], device_id={"gx": target}, device_id_type=MESH,
@@ -204,41 +208,40 @@
     for c in halo:
         c.start()
 
+    for c in sends:
+        c.wait_recv()
+
+    def grow(g, row, half):
+        lanes = pl.ds(pl.multiple_of(row * 256 + half * 128, 128), 128)
+        slots = pl.ds(pl.multiple_of(g * 8, 8), 8)
+        at = g * 512 + half * 16 + row
+        heat_in = 0.2 * (rcv[pl.ds(at, 8, stride=64), :] + 1.8)
+        cool_in = 0.2 * rcv[pl.ds(at + 32, 8, stride=64), :]
+        mass = jnp.zeros((8, 128), F32)
+        for c in range(NCAT):
+            change = cool_in * rc[c, slots, lanes] - heat_in
+            grown = jnp.maximum(thick[c, slots, lanes] + change, 0.0)
+            mass = mass + area[c, slots, lanes] * grown
+            nt[c, slots, lanes] = pres[c, slots, lanes].astype(F32) * grown
+        smass[pl.ds(g * 256 + half * 16 + row, 8, stride=32), :] = mass
+
+    @pl.loop(0, 32)
+    def _(i):
+        for k in range(2):
+            for half in range(2):
+                grow(i // 8, (i % 8) * 2 + k, half)
+
+    masses = [back(smass, rmass, mass_s, mass_r, i) for i in range(15)]
+    for c in masses:
+        c.start()
     stores = []
-    masses = [back(smass, rmass, mass_s, mass_r, i) for i in range(15)]
-
-    for dz in range(4):
-        group = (z + 4 - dz) % 4
-        for i in range(15):
-            if STEPS[i][0] == dz:
-                sends[i].wait_recv()
-
-        def grow(row, half):
-            lanes = pl.ds(pl.multiple_of(row * 256 + half * 128, 128), 128)
-            slots = pl.ds(pl.multiple_of(group * 8, 8), 8)
-            at = group * 512 + half * 16 + row
-            heat_in = 0.2 * (rcv[pl.ds(at, 8, stride=64), :] + 1.8)
-            cool_in = 0.2 * rcv[pl.ds(at + 32, 8, stride=64), :]
-            mass = jnp.zeros((8, 128), F32)
-            for c in range(NCAT):
-                change = cool_in * rc[c, slots, lanes] - heat_in
-                grown = jnp.maximum(thick[c, slots, lanes] + change, 0.0)
-                mass = mass + area[c, slots, lanes] * grown
-                nt[c, slots, lanes] = pres[c, slots, lanes].astype(F32) * grown
-            smass[pl.ds(group * 256 + half * 16 + row, 8, stride=32), :] = mass
-
-        @pl.loop(0, 16)
-        def _(row):
-            for half in range(2):
-                grow(row, half)
-
-        for i in range(15):
-            if STEPS[i][0] == dz:
-                masses[i].start()
-        slots = pl.ds(pl.multiple_of(group * 8, 8), 8)
-        c = pltpu.make_async_copy(nt.at[:, slots], nt_hbm.at[:, slots], osem.at[dz])
+
+    def store(src, dst):
+        c = pltpu.make_async_copy(src, dst, osem.at[len(stores)])
         c.start()
         stores.append(c)
+
+    store(nt, nt_hbm)
     rmass[mine, :] = smass[mine, :]
     s1s = [back(ss1, rs1, s1_s, s1_r, i) for i in range(15)]
 
@@ -352,7 +355,7 @@
 
     for c in halo:
         c.wait_send()
-    R = 8
+    R = 288
     wide = lax.broadcasted_iota(jnp.int32, (R, 128), 1)
     is_last, is_first = wide == 127, wide == 0
 
@@ -410,11 +413,6 @@
             outb[1, t, raw, :] = 0.5 * (a - b)
             outb[2, t, raw, :] = 0.5 * S[H, t, at, :]
 
-    def store(src, dst):
-        c = pltpu.make_async_copy(src, dst, osem.at[len(stores)])
-        c.start()
-        stores.append(c)
-
     for t in range(2):
         lanes = pl.ds(t * 128, 128)
         store(S.at[pl.ds(U, 2), t, pl.ds(OWN, 256)], velo_hbm.at[:, :, lanes])
@@ -440,18 +438,35 @@
         c.wait()
 
 
+def hand_over(nt, flux, velo, stro, nt_out, flux_out, velo_out, stro_out, nt_v, flux_v, velo_v, stro_v, sem):
+    parts = [(nt.at[c], nt_v.at[c], nt_out.at[c]) for c in range(NCAT)]
+    parts += [(stro.at[c], stro_v.at[c], stro_out.at[c]) for c in range(3)]
+    parts += [(velo.at[c], velo_v.at[c], velo_out.at[c]) for c in range(2)]
+    parts += [(flux.at[c], flux_v.at[c], flux_out.at[c]) for c in range(2)]
+    reads = [pltpu.make_async_copy(a, v, sem.at[0, i]) for i, (a, v, _) in enumerate(parts)]
+    writes = [pltpu.make_async_copy(v, b, sem.at[1, i]) for i, (_, v, b) in enumerate(parts)]
+    for c in reads:
+        c.start()
+    for c, d in zip(reads, writes):
+        c.wait()
+        d.start()
+    for d in writes:
+        d.wait()
+
+
 def local(sea, air, cur, wind, land, vel, stress, owner, thick, area, pres):
     any_ = pl.BlockSpec(memory_space=pl.ANY)
     vm = lambda *shape, dtype=F32: pltpu.VMEM(shape, dtype)
     dma = lambda n: pltpu.SemaphoreType.DMA((n,))
-    nt, flux, velo, stro = pl.pallas_call(
+    results = (
+        jax.ShapeDtypeStruct((NCAT, 32, 4096), F32),
+        jax.ShapeDtypeStruct((2, 256, 256), F32),
+        jax.ShapeDtypeStruct((2, 256, 256), F32),
+        jax.ShapeDtypeStruct((3, 256, 256), F32),
+    )
+    made = pl.pallas_call(
         kernel,
-        out_shape=(
-            jax.ShapeDtypeStruct((NCAT, 32, 4096), F32),
-            jax.ShapeDtypeStruct((2, 256, 256), F32),
-            jax.ShapeDtypeStruct((2, 256, 256), F32),
-            jax.ShapeDtypeStruct((3, 256, 256), F32),
-        ),
+        out_shape=results,
         in_specs=[pl.BlockSpec(memory_space=pltpu.SMEM)] + [any_] * 10,
         out_specs=(any_,) * 4,
         scratch_shapes=[
@@ -473,12 +488,20 @@
             dma(8), dma(8), dma(8), dma(8),
         ],
         compiler_params=pltpu.CompilerParams(
-            collective_id=0, has_side_effects=True, vmem_limit_bytes=48 * 1024 * 1024
+            collective_id=0, has_side_effects=True, vmem_limit_bytes=60 * 1024 * 1024
         ),
     )(
         owner, sea.reshape(16, 16, 256), air.reshape(16, 16, 256), cur, wind, land, vel, stress,
         thick.reshape(NCAT, 32, 4096), area.reshape(NCAT, 32, 4096), pres.reshape(NCAT, 32, 4096),
     )
+    nt, flux, velo, stro = pl.pallas_call(
+        hand_over,
+        out_shape=results,
+        in_specs=[any_] * 4,
+        out_specs=(any_,) * 4,
+        scratch_shapes=[vm(*o.shape) for o in results] + [pltpu.SemaphoreType.DMA((2, 12))],
+        compiler_params=pltpu.CompilerParams(vmem_limit_bytes=60 * 1024 * 1024),
+    )(*made)
     return nt.reshape(NCAT, 1, 32, 4096), flux, velo, stro
 
 

time: 119 us -> 66.1 us (0.56)
  Pallas kernels: 103 us -> 65.3 us
  local copies, waits for them, and re-layouts: 13.7 us -> 0 us
    pallas_call x1 -> x2, Pallas kernels: 103 us -> 65.3 us  [the longest x1 61.5 us: local(): pl.pallas_call(kernel, out_shape=results, in_specs=[pl.BlockSpec(memory_s...]
    unnamed x20 -> x0, local copies, waits for them, and re-layouts: 13.7 us -> none
where the time goes in v2:
time: 66.1 us; the launch traced here: 66 us
  Pallas kernels  65.3 us (99%)
    pallas_call x1, Pallas kernels, local(): pl.pallas_call(kernel, out_shape=results, in_specs=[pl.BlockSpec(memory_s...  61.5 us
    pallas_call x1, Pallas kernels, local(): pl.pallas_call(hand_over, out_shape=results, in_specs=[any_] * 4, out_spe...  3.81 us

profile of v2, /device:TPU:1, one launch (start us, length us, event | category | flops | bytes accessed | tf_op | source)
XLA Modules:
  0.0 66.0 jit_solution(10274393704202967969)
XLA Ops:
  0.6 61.5 %shard_map.138 = (f32[5,32,4096]{2,1,0:T(8,128)}, f32[2,256,256]{2,1,0:T(8,128)}, f32[2,256,256]{2,1,0:T(8,128)}, f32[3,256,256]{2,1,0:T(8,128)}) custom-call(s32[1,16]{1,0:T(1,128)} %owner_ref.1, f32[16,16,256]{2,1,0:T(8,128)} %bitcast.11, f32[16,16,256]{2,1,0:T(8,128)} %bitcast.12, f32[2,256,256]{2,1,0:T(8,128)} %cur_hbm.1, f32[2,256,256]{2,1,0:T(8,128)} %wind_hbm.1, ...), custom_call_target="tpu_custom_call" | custom-call | tf_op jit(solution)/shard_map/pallas_call | solution.py:467
  62.2 3.8 %shard_map.139 = (f32[5,32,4096]{2,1,0:T(8,128)}, f32[2,256,256]{2,1,0:T(8,128)}, f32[2,256,256]{2,1,0:T(8,128)}, f32[3,256,256]{2,1,0:T(8,128)}) custom-call(f32[5,32,4096]{2,1,0:T(8,128)} %get-tuple-element.12.nt, f32[2,256,256]{2,1,0:T(8,128)} %get-tuple-element.13.flux, f32[2,256,256]{2,1,0:T(8,128)} %get-tuple-element.14.velo, ...), custom_call_target="tpu_custom_call" | custom-call | tf_op jit(solution)/shard_map/pallas_call | solution.py:497

commit v3 on v2

--- a/solution.py
+++ b/solution.py
@@ -50,6 +50,15 @@
 
     load("sea", sea_hbm, sea)
     load("air", air_hbm, air)
+    barrier = pltpu.get_barrier_semaphore()
+    north, south = (r + 1) % 8, (r + 7) % 8
+    east, west = (s + 1) % 16, (s + 15) % 16
+    for dz, dx in STEPS:
+        pl.semaphore_signal(barrier, inc=1, device_id={"gx": dev(dz, dx)}, device_id_type=MESH)
+    for ry in (north, south):
+        for sx in (west, s, east):
+            pl.semaphore_signal(barrier, inc=1, device_id={"gy": ry, "gx": sx}, device_id_type=MESH)
+
     load("thick", thick_hbm, thick)
     load("area", area_hbm, area)
     load("pres", pres_hbm, pres)
@@ -60,15 +69,6 @@
         load(("wind", t), wind_hbm.at[:, :, lanes], wind.at[:, t])
         load(("cur", t), cur_hbm.at[:, :, lanes], cur.at[:, t])
         load(("land", t), land_hbm.at[:, lanes], land.at[t])
-
-    barrier = pltpu.get_barrier_semaphore()
-    north, south = (r + 1) % 8, (r + 7) % 8
-    east, west = (s + 1) % 16, (s + 15) % 16
-    for dz, dx in STEPS:
-        pl.semaphore_signal(barrier, inc=1, device_id={"gx": dev(dz, dx)}, device_id_type=MESH)
-    for ry in (north, south):
-        for sx in (west, s, east):
-            pl.semaphore_signal(barrier, inc=1, device_id={"gy": ry, "gx": sx}, device_id_type=MESH)
 
     owners = [owner_ref[0, b] for b in range(NBLK)]
     spare = jnp.zeros((8, 128), F32)
@@ -322,10 +322,26 @@
     ]
     for c in halo_m:
         c.start()
-    for c in s1s:
-        c.start()
+
+    def coefficients(t, row0, rows):
+        at = pl.ds(row0, rows)
+        inertia = M[0, t, at, :] + 0.5
+        w = S[WET, t, at, :] / (inertia + 0.24)
+        cA[t, at, :] = w * inertia
+        cB[t, at, :] = 0.075 * w
+        cG[0, t, at, :] = 0.3 * w * S[FU, t, at, :]
+        cG[1, t, at, :] = 0.3 * w * S[FV, t, at, :]
+        cK[t, at, :] = M[1, t, at, :] * (1.0 / 6.0)
+
+    @pl.loop(0, 4)
+    def _(i):
+        for t in range(2):
+            coefficients(t, pl.multiple_of(OWN + i * 64, 8), 64)
+
     for c in halo_m:
         c.wait_recv()
+    for c in s1s:
+        c.start()
     for f in range(2):
         for chunk in range(4):
             k = 32 * chunk + 16 * f
@@ -341,17 +357,13 @@
             M[f, 2, pl.ds(280 + i * 8, 8), :] = beside(KR[1, raw, :], KL[1, raw, :], (128 - k) % 128, 112 - k)
     clear_outside(M, 2)
 
-    @pl.loop(1, 37)
-    def _(i):
-        at = pl.ds(pl.multiple_of(i * 8, 8), 8)
-        for t in range(3):
-            inertia = M[0, t, at, :] + 0.5
-            w = S[WET, t, at, :] / (inertia + 0.24)
-            cA[t, at, :] = w * inertia
-            cB[t, at, :] = 0.075 * w
-            cG[0, t, at, :] = 0.3 * w * S[FU, t, at, :]
-            cG[1, t, at, :] = 0.3 * w * S[FV, t, at, :]
-            cK[t, at, :] = M[1, t, at, :] * (1.0 / 6.0)
+    for t in range(2):
+        coefficients(t, 8, 16)
+        coefficients(t, 280, 16)
+
+    @pl.loop(0, 4)
+    def _(i):
+        coefficients(2, pl.multiple_of(8 + i * 72, 8), 72)
 
     for c in halo:
         c.wait_send()
@@ -403,10 +415,10 @@
                 S[U, t, at, :] = a * S[U, t, at, :] + (b * fe + cG[0, t, at, :])
                 S[V, t, at, :] = a * S[V, t, at, :] + (b * fn + cG[1, t, at, :])
 
-    @pl.loop(0, 32)
-    def _(i):
-        at = own_rows(i)
-        raw = pl.ds(pl.multiple_of(i * 8, 8), 8)
+    @pl.loop(0, 4)
+    def _(i):
+        at = pl.ds(pl.multiple_of(OWN + i * 64, 8), 64)
+        raw = pl.ds(pl.multiple_of(i * 64, 8), 64)
         for t in range(2):
             a, b = S[X, t, at, :], S[Y, t, at, :]
             outb[0, t, raw, :] = 0.5 * (a + b)

time: 66.1 us -> 63.6 us (0.962)
  Pallas kernels: 65.3 us -> 62.8 us
    pallas_call x1, Pallas kernels: 61.5 us -> 59 us  [local(): pl.pallas_call(kernel, out_shape=results, in_specs=[pl.BlockSpec(memory_s...]
where the time goes in v3:
time: 63.6 us; the launch traced here: 63.4 us
  Pallas kernels  62.8 us (99%)
  between operations  0.64 us (1%)
    pallas_call x1, Pallas kernels, local(): pl.pallas_call(kernel, out_shape=results, in_specs=[pl.BlockSpec(memory_s...  59 us
    pallas_call x1, Pallas kernels, local(): pl.pallas_call(hand_over, out_shape=results, in_specs=[any_] * 4, out_spe...  3.81 us

profile of v3, /device:TPU:1, one launch (start us, length us, event | category | flops | bytes accessed | tf_op | source)
XLA Modules:
  0.0 63.4 jit_solution(14976118474572694014)
XLA Ops:
  0.6 59.0 %shard_map.138 = (f32[5,32,4096]{2,1,0:T(8,128)}, f32[2,256,256]{2,1,0:T(8,128)}, f32[2,256,256]{2,1,0:T(8,128)}, f32[3,256,256]{2,1,0:T(8,128)}) custom-call(s32[1,16]{1,0:T(1,128)} %owner_ref.1, f32[16,16,256]{2,1,0:T(8,128)} %bitcast.11, f32[16,16,256]{2,1,0:T(8,128)} %bitcast.12, f32[2,256,256]{2,1,0:T(8,128)} %cur_hbm.1, f32[2,256,256]{2,1,0:T(8,128)} %wind_hbm.1, ...), custom_call_target="tpu_custom_call" | custom-call | tf_op jit(solution)/shard_map/pallas_call | solution.py:479
  59.6 3.8 %shard_map.139 = (f32[5,32,4096]{2,1,0:T(8,128)}, f32[2,256,256]{2,1,0:T(8,128)}, f32[2,256,256]{2,1,0:T(8,128)}, f32[3,256,256]{2,1,0:T(8,128)}) custom-call(f32[5,32,4096]{2,1,0:T(8,128)} %get-tuple-element.12.nt, f32[2,256,256]{2,1,0:T(8,128)} %get-tuple-element.13.flux, f32[2,256,256]{2,1,0:T(8,128)} %get-tuple-element.14.velo, ...), custom_call_target="tpu_custom_call" | custom-call | tf_op jit(solution)/shard_map/pallas_call | solution.py:509

commit v4 on v3

--- a/solution.py
+++ b/solution.py
@@ -279,22 +279,29 @@
         slot_of.append(slot)
     for c in covs:
         c.wait_recv()
+    for k in range(32):
+        got[1, k] = rcov[pl.ds(k * 32, 32), :]
+    for b in range(NBLK):
+        cover = got[1, slot_of[b]]
+        damping = jnp.exp(-2.0 * (1.0 - cover))
+        temp_b, cool_b = sea[b], air[b]
+        for half in range(2):
+            part = slice(half * 16, half * 16 + 16)
+            lanes = slice(half * 128, half * 128 + 128)
+            cv = cover[part]
+            M[1, half, pl.ds(OWN + b * 16, 16), :] = damping[part]
+            flux[0, half, pl.ds(b * 16, 16), :] = cv * (0.5 * (temp_b[:, lanes] + 1.8)) - (1.0 - cv) * cool_b[:, lanes]
     for c in masses:
         c.wait_recv()
     for k in range(32):
         got[0, k] = rmass[pl.ds(k * 32, 32), :]
-        got[1, k] = rcov[pl.ds(k * 32, 32), :]
     for b in range(NBLK):
-        mass, cover = got[0, slot_of[b]], got[1, slot_of[b]]
-        strength = mass * jnp.exp(-2.0 * (1.0 - cover))
-        temp_b, cool_b = sea[b], air[b]
+        mass = got[0, slot_of[b]]
         for half in range(2):
-            part = slice(half * 16, half * 16 + 16)
-            lanes = slice(half * 128, half * 128 + 128)
-            M[0, half, pl.ds(OWN + b * 16, 16), :] = mass[part]
-            M[1, half, pl.ds(OWN + b * 16, 16), :] = strength[part]
-            cv = cover[part]
-            flux[0, half, pl.ds(b * 16, 16), :] = cv * (0.5 * (temp_b[:, lanes] + 1.8)) - (1.0 - cv) * cool_b[:, lanes]
+            rows = pl.ds(OWN + b * 16, 16)
+            part = mass[half * 16 : half * 16 + 16]
+            M[0, half, rows, :] = part
+            M[1, half, rows, :] = M[1, half, rows, :] * part
 
     for i in range(8):
         left = jnp.zeros((8, 128), F32)
@@ -338,9 +345,57 @@
         for t in range(2):
             coefficients(t, pl.multiple_of(OWN + i * 64, 8), 64)
 
+    def across(f, row0, rows, tiles):
+        wide = lax.broadcasted_iota(jnp.int32, (rows, 128), 1)
+        v = [S[f, t, pl.ds(row0, rows), :] for t in range(3)]
+        up = [pltpu.roll(a, 127, 1) for a in v]
+        down = [pltpu.roll(a, 1, 1) for a in v]
+        return {
+            t: jnp.where(wide == 127, up[(t + 1) % 3], up[t]) - jnp.where(wide == 0, down[(t + 2) % 3], down[t])
+            for t in tiles
+        }
+
+    def along(f, t, row0, rows):
+        return S[f, t, pl.ds(row0 + 1, rows), :] - S[f, t, pl.ds(row0 - 1, rows), :]
+
+    def relax(row0, rows, tiles=(0, 1, 2)):
+        at = pl.ds(row0, rows)
+        ux, vx = across(U, row0, rows, tiles), across(V, row0, rows, tiles)
+        for t in tiles:
+            a, b = ux[t], along(V, t, row0, rows)
+            sh = along(U, t, row0, rows) + vx[t]
+            d, e = a + b, a - b
+            k = cK[t, at, :]
+            d4 = 4.0 * d
+            q = d * d4 + e * e + (sh * sh + 0.64)
+            f = k * lax.rsqrt(q)
+            k2 = k + k
+            S[X, t, at, :] = S[X, t, at, :] * (1.0 / 1.5) + (f * (d4 + e) - k2)
+            S[Y, t, at, :] = S[Y, t, at, :] * (1.0 / 1.5) + (f * (d4 - e) - k2)
+            S[H, t, at, :] = S[H, t, at, :] * (1.0 / 1.5) + (f + f) * sh
+
+    def move(row0, rows, tiles=(0, 1, 2)):
+        at = pl.ds(row0, rows)
+        xx, hx = across(X, row0, rows, tiles), across(H, row0, rows, tiles)
+        for t in tiles:
+            a, b = cA[t, at, :], cB[t, at, :]
+            fe = xx[t] + along(H, t, row0, rows)
+            fn = hx[t] + along(Y, t, row0, rows)
+            S[U, t, at, :] = a * S[U, t, at, :] + (b * fe + cG[0, t, at, :])
+            S[V, t, at, :] = a * S[V, t, at, :] + (b * fn + cG[1, t, at, :])
+
+    for c in s1s[:8]:
+        c.start()
+    for c in halo:
+        c.wait_send()
+
+    @pl.loop(0, 4)
+    def _(i):
+        relax(pl.multiple_of(OWN + i * 64, 8), 64, (0, 1))
+
     for c in halo_m:
         c.wait_recv()
-    for c in s1s:
+    for c in s1s[8:]:
         c.start()
     for f in range(2):
         for chunk in range(4):
@@ -365,55 +420,22 @@
     def _(i):
         coefficients(2, pl.multiple_of(8 + i * 72, 8), 72)
 
-    for c in halo:
-        c.wait_send()
-    R = 288
-    wide = lax.broadcasted_iota(jnp.int32, (R, 128), 1)
-    is_last, is_first = wide == 127, wide == 0
-
-    def across(f, at):
-        v = [S[f, t, at, :] for t in range(3)]
-        up = [pltpu.roll(a, 127, 1) for a in v]
-        down = [pltpu.roll(a, 1, 1) for a in v]
-        return [
-            jnp.where(is_last, up[(t + 1) % 3], up[t]) - jnp.where(is_first, down[(t + 2) % 3], down[t])
-            for t in range(3)
-        ]
-
-    def along(f, t, row0):
-        return S[f, t, pl.ds(row0 + 1, R), :] - S[f, t, pl.ds(row0 - 1, R), :]
-
-    @pl.loop(0, NSUB)
+    for t in range(2):
+        relax(8, 16, (t,))
+        relax(280, 16, (t,))
+
+    @pl.loop(0, 3)
+    def _(i):
+        relax(pl.multiple_of(8 + i * 96, 8), 96, (2,))
+
+    @pl.loop(1, NSUB)
     def _(n):
-        @pl.loop(0, 288 // R)
-        def _(i):
-            row0 = pl.multiple_of(i * R + 8, 8)
-            at = pl.ds(row0, R)
-            ux, vx = across(U, at), across(V, at)
-            for t in range(3):
-                a, b = ux[t], along(V, t, row0)
-                sh = along(U, t, row0) + vx[t]
-                d, e = a + b, a - b
-                k = cK[t, at, :]
-                d4 = 4.0 * d
-                q = d * d4 + e * e + (sh * sh + 0.64)
-                f = k * lax.rsqrt(q)
-                k2 = k + k
-                S[X, t, at, :] = S[X, t, at, :] * (1.0 / 1.5) + (f * (d4 + e) - k2)
-                S[Y, t, at, :] = S[Y, t, at, :] * (1.0 / 1.5) + (f * (d4 - e) - k2)
-                S[H, t, at, :] = S[H, t, at, :] * (1.0 / 1.5) + (f + f) * sh
-
-        @pl.loop(0, 288 // R)
-        def _(i):
-            row0 = pl.multiple_of(i * R + 8, 8)
-            at = pl.ds(row0, R)
-            xx, hx = across(X, at), across(H, at)
-            for t in range(3):
-                a, b = cA[t, at, :], cB[t, at, :]
-                fe = xx[t] + along(H, t, row0)
-                fn = hx[t] + along(Y, t, row0)
-                S[U, t, at, :] = a * S[U, t, at, :] + (b * fe + cG[0, t, at, :])
-                S[V, t, at, :] = a * S[V, t, at, :] + (b * fn + cG[1, t, at, :])
+        move(8, 288)
+        relax(8, 288)
+
+    @pl.loop(0, 4)
+    def _(i):
+        move(pl.multiple_of(OWN + i * 64, 8), 64, (0, 1))
 
     @pl.loop(0, 4)
     def _(i):

time: 63.6 us -> 64.2 us (level)
  no operation moved by 1% of the time
where the time goes in v4:
time: 64.2 us; the launch traced here: 64 us
  Pallas kernels  63.4 us (99%)
    pallas_call x1, Pallas kernels, local(): pl.pallas_call(kernel, out_shape=results, in_specs=[pl.BlockSpec(memory_s...  59.6 us
    pallas_call x1, Pallas kernels, local(): pl.pallas_call(hand_over, out_shape=results, in_specs=[any_] * 4, out_spe...  3.81 us

profile of v4, /device:TPU:1, one launch (start us, length us, event | category | flops | bytes accessed | tf_op | source)
XLA Modules:
  0.0 64.0 jit_solution(3384530548263055344)
XLA Ops:
  0.6 59.6 %shard_map.138 = (f32[5,32,4096]{2,1,0:T(8,128)}, f32[2,256,256]{2,1,0:T(8,128)}, f32[2,256,256]{2,1,0:T(8,128)}, f32[3,256,256]{2,1,0:T(8,128)}) custom-call(s32[1,16]{1,0:T(1,128)} %owner_ref.1, f32[16,16,256]{2,1,0:T(8,128)} %bitcast.11, f32[16,16,256]{2,1,0:T(8,128)} %bitcast.12, f32[2,256,256]{2,1,0:T(8,128)} %cur_hbm.1, f32[2,256,256]{2,1,0:T(8,128)} %wind_hbm.1, ...), custom_call_target="tpu_custom_call" | custom-call | tf_op jit(solution)/shard_map/pallas_call | solution.py:501
  60.2 3.8 %shard_map.139 = (f32[5,32,4096]{2,1,0:T(8,128)}, f32[2,256,256]{2,1,0:T(8,128)}, f32[2,256,256]{2,1,0:T(8,128)}, f32[3,256,256]{2,1,0:T(8,128)}) custom-call(f32[5,32,4096]{2,1,0:T(8,128)} %get-tuple-element.12.nt, f32[2,256,256]{2,1,0:T(8,128)} %get-tuple-element.13.flux, f32[2,256,256]{2,1,0:T(8,128)} %get-tuple-element.14.velo, ...), custom_call_target="tpu_custom_call" | custom-call | tf_op jit(solution)/shard_map/pallas_call | solution.py:531

commit v5 on v4

--- a/solution.py
+++ b/solution.py
@@ -37,8 +37,8 @@
 
     odd = r % 2
 
-    def dev(dz, dx):
-        dz, dx = dz + odd * (dx - dz), dx + odd * (dz - dx)
+    def dev(dz, dx, exchange=odd):
+        dz, dx = dz + exchange * (dx - dz), dx + exchange * (dz - dx)
         return ((z + dz) % 4) * 4 + (x + dx) % 4
 
     loads = {}
@@ -138,9 +138,9 @@
         for half in range(2):
             prepare(i // 16, i % 16, half)
 
-    def back(buf, dst, ssem, rsem, i):
+    def back(buf, dst, ssem, rsem, i, exchange=odd):
         dz, dx = STEPS[i]
-        target = dev(-dz, -dx)
+        target = dev(-dz, -dx, exchange)
         return pltpu.make_async_remote_copy(
             src_ref=buf.at[pl.ds(pl.multiple_of(target * 64, 64), 64)],
             dst_ref=dst.at[pl.ds(pl.multiple_of(s * 64, 64), 64)],
@@ -225,15 +225,19 @@
             nt[c, slots, lanes] = pres[c, slots, lanes].astype(F32) * grown
         smass[pl.ds(g * 256 + half * 16 + row, 8, stride=32), :] = mass
 
-    @pl.loop(0, 32)
-    def _(i):
-        for k in range(2):
-            for half in range(2):
-                grow(i // 8, (i % 8) * 2 + k, half)
-
-    masses = [back(smass, rmass, mass_s, mass_r, i) for i in range(15)]
-    for c in masses:
-        c.start()
+    masses = [back(smass, rmass, mass_s, mass_r, i, 0) for i in range(15)]
+    for dz in range(4):
+        group = (z + 4 - dz) % 4
+
+        @pl.loop(0, 8)
+        def _(i):
+            for k in range(2):
+                for half in range(2):
+                    grow(group, i * 2 + k, half)
+
+        for i in range(15):
+            if STEPS[i][0] == dz:
+                masses[i].start()
     stores = []
 
     def store(src, dst):
@@ -384,8 +388,6 @@
             S[U, t, at, :] = a * S[U, t, at, :] + (b * fe + cG[0, t, at, :])
             S[V, t, at, :] = a * S[V, t, at, :] + (b * fn + cG[1, t, at, :])
 
-    for c in s1s[:8]:
-        c.start()
     for c in halo:
         c.wait_send()
 
@@ -395,7 +397,7 @@
 
     for c in halo_m:
         c.wait_recv()
-    for c in s1s[8:]:
+    for c in s1s:
         c.start()
     for f in range(2):
         for chunk in range(4):

time: 64.2 us -> 63 us (0.981)
  Pallas kernels: 63.4 us -> 62.2 us
    pallas_call x1, Pallas kernels: 59.6 us -> 58.4 us  [local(): pl.pallas_call(kernel, out_shape=results, in_specs=[pl.BlockSpec(memory_s...]
where the time goes in v5:
time: 63 us; the launch traced here: 62.8 us
  Pallas kernels  62.2 us (99%)
  between operations  0.64 us (1%)
    pallas_call x1, Pallas kernels, local(): pl.pallas_call(kernel, out_shape=results, in_specs=[pl.BlockSpec(memory_s...  58.4 us
    pallas_call x1, Pallas kernels, local(): pl.pallas_call(hand_over, out_shape=results, in_specs=[any_] * 4, out_spe...  3.81 us

profile of v5, /device:TPU:1, one launch (start us, length us, event | category | flops | bytes accessed | tf_op | source)
XLA Modules:
  0.0 62.8 jit_solution(7525488354954460197)
XLA Ops:
  0.6 58.4 %shard_map.138 = (f32[5,32,4096]{2,1,0:T(8,128)}, f32[2,256,256]{2,1,0:T(8,128)}, f32[2,256,256]{2,1,0:T(8,128)}, f32[3,256,256]{2,1,0:T(8,128)}) custom-call(s32[1,16]{1,0:T(1,128)} %owner_ref.1, f32[16,16,256]{2,1,0:T(8,128)} %bitcast.11, f32[16,16,256]{2,1,0:T(8,128)} %bitcast.12, f32[2,256,256]{2,1,0:T(8,128)} %cur_hbm.1, f32[2,256,256]{2,1,0:T(8,128)} %wind_hbm.1, ...), custom_call_target="tpu_custom_call" | custom-call | tf_op jit(solution)/shard_map/pallas_call | solution.py:503
  59.0 3.8 %shard_map.139 = (f32[5,32,4096]{2,1,0:T(8,128)}, f32[2,256,256]{2,1,0:T(8,128)}, f32[2,256,256]{2,1,0:T(8,128)}, f32[3,256,256]{2,1,0:T(8,128)}) custom-call(f32[5,32,4096]{2,1,0:T(8,128)} %get-tuple-element.12.nt, f32[2,256,256]{2,1,0:T(8,128)} %get-tuple-element.13.flux, f32[2,256,256]{2,1,0:T(8,128)} %get-tuple-element.14.velo, ...), custom_call_target="tpu_custom_call" | custom-call | tf_op jit(solution)/shard_map/pallas_call | solution.py:533
